TPU v7x, 32 devices: a whole 2x2x4 slice. The times are simulated.
32 devices in a mesh: grp: 2 (over y), chan: 2 (over x), tm: 4 (over z), pol: 2 (over core).
Axes of the slice: x: 2, y: 2, z: 4, core: 2. Of those that a mesh axis runs over, the one named last changes fastest.
Arguments:
- voltages: bfloat16 [4, 2, 256, 32768], P('grp', 'pol', 'chan', 'tm'), parts along dimension 0, may hold values from -6 to 6
- taps_filter: float32 [16, 2048], replicated, may hold values from -1.5 to 1.5
- tile_a: int32 [14, 64], replicated, may hold values from 0 to 255
- tile_b: int32 [14, 64], replicated, may hold values from 0 to 255
- tile_owner: int32 [14], replicated, may hold values from 0 to 1, as said below
- tile_flags: int32 [14, 16], replicated, may hold values 0 or 1
Outputs:
- visibility: float32 [16, 256, 4, 2, 64, 128], P('pol', ('chan', 'tm'), 'grp'), parts along dimension 2
There are 2 independent parts, one for each index of `grp`. A program takes and returns all parts, laid end to end along the dimension named above; an argument that names none is the same for every part. Nothing has to cross between parts.
Inputs may be any that keep to these rules, and one draw needn't show every extreme that they name: `tile_owner`: one owner holds exactly 8 tiles and the other owner holds all the rest.
All inputs are finite; a program needn't handle non-finite values.
Results may differ from a plain program's by a relative error of at most 0.0035.
Values may be sent and summed in bfloat16 or wider, within the bound.
A program may use at most 128 MiB of HBM per device.

v0:
```python
import math

import jax
import ml_dtypes
import numpy as np
import jax.numpy as jnp
from jax import lax
from jax.experimental import pallas as pl
from jax.experimental.pallas import tpu as pltpu
from jax.sharding import PartitionSpec as P

AVG = 8
CAP = 8

radix_first = 16


def fourier(filtered):
    length = filtered.shape[-1]
    second = length // radix_first
    mode = lax.Precision.HIGH
    grid = filtered.reshape(filtered.shape[:-1] + (radix_first, second))
    outer = jnp.arange(radix_first, dtype=jnp.int32)
    inner = jnp.arange(second, dtype=jnp.int32)
    phase_one = (
        2.0
        * math.pi
        / radix_first
        * (outer[:, None] * outer[None, :] % radix_first).astype(jnp.float32)
    )
    phase_twist = 2.0 * math.pi / length * (outer[:, None] * inner[None, :]).astype(jnp.float32)
    phase_two = (
        2.0 * math.pi / second * (inner[:, None] * inner[None, :] % second).astype(jnp.float32)
    )
    scale = 1.0 / math.sqrt(length)
    cos_one, sin_one = (jnp.cos(phase_one), jnp.sin(phase_one))
    cos_twist, sin_twist = (jnp.cos(phase_twist), jnp.sin(phase_twist))
    cos_two, sin_two = (jnp.cos(phase_two) * scale, jnp.sin(phase_two) * scale)
    one = jnp.stack([jnp.stack([cos_one, sin_one]), jnp.stack([-sin_one, cos_one])])
    two = jnp.stack([jnp.stack([cos_two, sin_two]), jnp.stack([-sin_two, cos_two])])
    section = jnp.einsum("qrfk,rnkj->qnfj", one, grid, precision=mode)
    turned = jnp.stack(
        [
            section[0] * cos_twist + section[1] * sin_twist,
            section[1] * cos_twist - section[0] * sin_twist,
        ]
    )
    return jnp.einsum("qrgj,rnfj->qngf", two, turned, precision=mode)


def times(value, angle):
    re, im = value
    if angle % 16 == 0:
        return re, im
    c, s = math.cos(2.0 * math.pi * angle / 16), math.sin(2.0 * math.pi * angle / 16)
    if angle % 16 == 4:
        return im, -re
    return re * c + im * s, im * c - re * s


def four(x):
    plus = [x[0][i] + x[2][i] for i in range(2)]
    minus = [x[0][i] - x[2][i] for i in range(2)]
    plus_odd = [x[1][i] + x[3][i] for i in range(2)]
    minus_odd = [x[1][i] - x[3][i] for i in range(2)]
    return [
        (plus[0] + plus_odd[0], plus[1] + plus_odd[1]),
        (minus[0] + minus_odd[1], minus[1] - minus_odd[0]),
        (plus[0] - plus_odd[0], plus[1] - plus_odd[1]),
        (minus[0] - minus_odd[1], minus[1] + minus_odd[0]),
    ]


def sixteen(x):
    inner = [four([x[4 * a + b] for a in range(4)]) for b in range(4)]
    result = [None] * 16
    for c in range(4):
        ends = four([times(inner[b][c], b * c) for b in range(4)])
        for d in range(4):
            result[c + 4 * d] = ends[d]
    return result


def spectra_kernel(x_ref, taps_ref, cos_ref, sin_ref, high_ref, low_ref, out_ref, held, turned):
    time_count, block = x_ref.shape[1:3]
    taps, length = taps_ref.shape
    frames = x_ref.shape[3] // length
    spectra_count = time_count * frames
    second = length // radix_first
    depth = AVG * spectra_count

    def filter_section(k1, carry):
        at = pl.multiple_of(k1 * second, second)
        rows = [taps_ref[m : m + 1, pl.ds(at, second)] for m in range(taps)]
        for r in range(2):
            samples = []
            for t in range(spectra_count):
                place = pl.multiple_of(k1 * second + (t % frames) * length, second)
                samples.append(x_ref[r, t // frames, :, pl.ds(place, second)].astype(jnp.float32))
            filtered = []
            for t in range(spectra_count):
                total = rows[0] * samples[t]
                for m in range(1, min(taps, t + 1)):
                    total = total + rows[m] * samples[t - m]
                filtered.append(total)
            held[r, :, :, pl.ds(at, second)] = jnp.transpose(jnp.stack(filtered), (1, 0, 2))
        return carry

    lax.fori_loop(0, radix_first, filter_section, 0)

    def transform_station(s, carry):
        sections = [
            tuple(held[r, s, :, k1 * second : (k1 + 1) * second] for r in range(2))
            for k1 in range(radix_first)
        ]
        rows = []
        for f1, (re, im) in enumerate(sixteen(sections)):
            c, n = cos_ref[f1 : f1 + 1, :], sin_ref[f1 : f1 + 1, :]
            rows.append(jnp.concatenate([re * c + im * n, im * c - re * n], axis=-1))
        joined = jnp.concatenate(rows, axis=0)
        high = joined.astype(jnp.bfloat16)
        low = (joined - high.astype(jnp.float32)).astype(jnp.bfloat16)

        def product(matrix, data):
            return lax.dot_general(
                matrix, data, (((1,), (1,)), ((), ())), preferred_element_type=jnp.float32
            )

        turned[s] = (
            product(high_ref[...], high)
            + product(high_ref[...], low)
            + product(low_ref[...], high)
        )
        return carry

    lax.fori_loop(0, block, transform_station, 0)

    def place_channels(f, carry):
        at = pl.multiple_of(f * 16, 16)
        for q in range(2):
            for h in range(radix_first // AVG):
                part = turned[:, pl.ds(q * second + at, 16), h * depth : (h + 1) * depth]
                out_ref[pl.ds(at, 16), h, q] = jnp.transpose(part, (1, 0, 2)).astype(jnp.bfloat16)
        return carry

    lax.fori_loop(0, second // 16, place_channels, 0)


def local_spectra(blocks, taps_filter):
    _, time_count, share, samples = blocks.shape
    taps, length = taps_filter.shape
    spectra_count = time_count * (samples // length)
    second = length // radix_first
    depth = AVG * spectra_count
    block = 16
    inner = np.arange(second)
    twist = 2.0 * np.pi / length * (np.arange(radix_first)[:, None] * inner[None, :])
    phase = 2.0 * np.pi / second * (inner[:, None] * inner[None, :] % second)
    c, s = np.cos(phase) / math.sqrt(length), np.sin(phase) / math.sqrt(length)
    matrix = np.block([[c, s], [-s, c]])
    high = matrix.astype(ml_dtypes.bfloat16)
    low = (matrix - high.astype(np.float64)).astype(ml_dtypes.bfloat16)
    whole = lambda shape: pl.BlockSpec(shape, lambda i: (0, 0))
    return pl.pallas_call(
        spectra_kernel,
        grid=(share // block,),
        in_specs=[
            pl.BlockSpec((2, time_count, block, samples), lambda i: (0, 0, i, 0)),
            whole((taps, length)),
            whole((radix_first, second)),
            whole((radix_first, second)),
            whole((2 * second, 2 * second)),
            whole((2 * second, 2 * second)),
        ],
        out_specs=pl.BlockSpec(
            (second, radix_first // AVG, 2, block, depth), lambda i: (0, 0, 0, i, 0)
        ),
        out_shape=jax.ShapeDtypeStruct(
            (second, radix_first // AVG, 2, share, depth), jnp.bfloat16
        ),
        scratch_shapes=[
            pltpu.VMEM((2, block, spectra_count, length), jnp.float32),
            pltpu.VMEM((block, 2 * second, radix_first * spectra_count), jnp.float32),
        ],
        compiler_params=pltpu.CompilerParams(vmem_limit_bytes=48 * 2**20),
    )(
        blocks,
        taps_filter,
        np.cos(twist).astype(np.float32),
        np.sin(twist).astype(np.float32),
        high,
        low,
    )


def plain_spectra(blocks, taps_filter):
    _, time_count, share, samples = blocks.shape
    taps, length = taps_filter.shape
    frames = samples // length
    spectra_count = time_count * frames
    blocks = blocks.reshape(2, time_count, share, frames, length)
    blocks = blocks.transpose(0, 2, 1, 3, 4).reshape(2, share, spectra_count, length)
    extended = jnp.pad(blocks, ((0, 0), (0, 0), (taps - 1, 0), (0, 0)))
    filtered = jnp.zeros((2, share, spectra_count, length), jnp.float32)
    for tap_index in range(taps):
        start = taps - 1 - tap_index
        filtered = filtered + taps_filter[tap_index] * extended[
            :, :, start : start + spectra_count
        ].astype(jnp.float32)
    spectra = fourier(filtered.reshape(2, share * spectra_count, length)).astype(jnp.bfloat16)
    outgoing = spectra.reshape(
        2, share, spectra_count, length // radix_first, radix_first // AVG, AVG
    )
    return outgoing.transpose(3, 4, 0, 1, 5, 2).reshape(
        length // radix_first, radix_first // AVG, 2, share, AVG * spectra_count
    )


def correlate_kernel(place_ref, rows_ref, weight_ref, own_ref, other_ref, out_ref, pick, source):
    sources, bands, parts, part_stations, depth = own_ref.shape
    stations = sources * part_stations
    capacity = out_ref.shape[0]
    width = out_ref.shape[4]

    @pl.when(pl.program_id(0) == 0)
    def _():
        columns = lax.broadcasted_iota(jnp.int32, pick.shape, 1)
        pick[...] = jnp.where(rows_ref[...] == columns, 1.0, 0.0).astype(jnp.bfloat16)

    for band in range(bands):
        for ref, polarisation in ((own_ref, place_ref[0]), (other_ref, 1 - place_ref[0])):
            at = pl.multiple_of(polarisation * (2 * depth), depth)
            source[band, :, pl.ds(at, 2 * depth)] = jnp.concatenate(
                [ref[:, band, r].reshape(stations, depth) for r in range(2)], axis=-1
            )
        picked = jnp.dot(pick[...], source[band], preferred_element_type=jnp.float32).astype(
            jnp.bfloat16
        )
        for slot in range(capacity):
            at = 2 * width * slot
            weight = weight_ref[slot]
            left = [
                picked[at : at + width, i * depth : (i + 1) * depth] * weight for i in range(4)
            ]
            other = picked[at + width : at + 2 * width]
            left_rows = jnp.concatenate(
                [
                    jnp.concatenate([left[0], left[1]], axis=-1),
                    jnp.concatenate([left[2], left[3]], axis=-1),
                    jnp.concatenate([left[1], -left[0]], axis=-1),
                    jnp.concatenate([left[3], -left[2]], axis=-1),
                ],
                axis=0,
            )
            right_rows = jnp.concatenate([other[:, : 2 * depth], other[:, 2 * depth :]], axis=0)
            result = lax.dot_general(
                left_rows,
                right_rows,
                (((1,), (1,)), ((), ())),
                preferred_element_type=jnp.float32,
            ) * (1.0 / depth)
            out_ref[slot, band] = result.reshape(2, 2, width, 2 * width)


def correlate(place, own, other, rows, weight):
    sources, bands, parts, part_stations, depth = own.shape
    width = rows.shape[1] // 2
    step = 2 if bands % 2 == 0 and bands > 2 else 1
    return pl.pallas_call(
        correlate_kernel,
        grid=(bands // step,),
        in_specs=[
            pl.BlockSpec(memory_space=pltpu.SMEM),
            pl.BlockSpec((CAP * 2 * width, 1), lambda g: (0, 0)),
            pl.BlockSpec((CAP, 1, depth), lambda g: (0, 0, 0)),
            pl.BlockSpec((sources, step, parts, part_stations, depth), lambda g: (0, g, 0, 0, 0)),
            pl.BlockSpec((sources, step, parts, part_stations, depth), lambda g: (0, g, 0, 0, 0)),
        ],
        out_specs=pl.BlockSpec(
            (CAP, step, 2, 2, width, 2 * width), lambda g: (0, g, 0, 0, 0, 0)
        ),
        out_shape=jax.ShapeDtypeStruct((CAP, bands, 2, 2, width, 2 * width), jnp.float32),
        scratch_shapes=[
            pltpu.VMEM((CAP * 2 * width, sources * part_stations), jnp.bfloat16),
            pltpu.VMEM((step, sources * part_stations, 4 * depth), jnp.bfloat16),
        ],
        compiler_params=pltpu.CompilerParams(vmem_limit_bytes=48 * 2**20),
    )(place, rows.reshape(CAP * 2 * width, 1), weight.astype(jnp.bfloat16), own, other)


def on_device(voltages, taps_filter, tile_a, tile_b, tile_owner, tile_flags):
    taps, length = taps_filter.shape
    stations = voltages.shape[2]
    frames = voltages.shape[3] // length
    chan_count = lax.axis_size("chan")
    time_count = lax.axis_size("tm")
    spectra_count = time_count * frames
    share = stations // time_count

    blocks = voltages.reshape(2, time_count, share, frames * length)
    blocks = lax.all_to_all(blocks, "tm", split_axis=1, concat_axis=1, tiled=True)
    spectra = (local_spectra if share % 16 == 0 else plain_spectra)(blocks, taps_filter)

    owners = chan_count * time_count
    bands = length // (owners * AVG)
    outgoing = spectra.reshape(owners, bands, 2, share, AVG * spectra_count)
    moved = lax.all_to_all(outgoing, ("chan", "tm"), split_axis=0, concat_axis=0, tiled=True)
    other = lax.ppermute(moved, "pol", [(0, 1), (1, 0)])

    position = lax.axis_index("pol")
    held = tile_owner == position
    rank = jnp.cumsum(held.astype(jnp.int32)) - 1
    chosen = (
        (rank[None, :] == jnp.arange(CAP, dtype=jnp.int32)[:, None]) & held[None, :]
    ).astype(jnp.int32)
    pairs = jnp.concatenate([tile_a, tile_b], axis=1)
    rows = jnp.sum(chosen[:, :, None] * pairs[None], axis=1)[:, :, None]
    flags = jnp.sum(chosen[:, :, None] * tile_flags[None], axis=1)
    weight = jnp.tile(flags.astype(jnp.float32), (1, AVG))[:, None, :]
    return correlate(position.reshape(1).astype(jnp.int32), moved, other, rows, weight)


def solution(mesh):
    return jax.shard_map(
        on_device,
        mesh=mesh,
        in_specs=(P("grp", "pol", "chan", "tm"), P(), P(), P(), P(), P()),
        out_specs=P("pol", ("chan", "tm"), "grp", None, None, None),
        check_vma=False,
    )
```

profile of v0, /device:TPU:0, one launch (start us, length us, event | category | flops | bytes accessed | tf_op | source)
XLA Modules:
  0.0 255.5 jit_solution(18003424966231885678)
XLA Ops:
  0.0 2.5 copy.20
  2.5 99.3 %all_to_all.10 = bf16[2,4,32,8192]{3,2,0,1:T(8,128)(2,1)S(1)} all-to-all(bf16[2,4,32,8192]{3,2,0,1:T(8,128)(2,1)S(1)} %copy.20), channel_id=1, replica_groups=mesh['grp'=2,'chan'=2,'tm'=4,'pol'=2] {'tm'}, dimensions={1} | all-to-all | bytes 8388608 | tf_op jit(solution)/shard_map/all_to_all | solution.py:301
  101.7 0.0 copy-start
  101.7 0.0 copy-start.1
  101.7 0.0 copy-start.2
  101.7 0.0 copy-start.3
  101.7 0.0 copy-start.4
  101.7 2.3 copy.21.x_ref
  104.0 0.0 copy-done
  104.0 0.0 copy-done.1
  104.0 0.0 copy-done.2
  104.0 0.0 copy-done.3
  104.0 0.0 copy-done.4
  104.1 21.7 %shard_map.100 = bf16[128,2,2,32,128]{4,3,2,1,0:T(8,128)(2,1)S(1)} custom-call(bf16[2,4,32,8192]{3,2,1,0:T(8,128)(2,1)} %copy.21.x_ref, f32[16,2048]{1,0:T(8,128)S(1)} %copy-done, f32[16,128]{1,0:T(8,128)S(1)} %copy-done.4, f32[16,128]{1,0:T(8,128)S(1)} %copy-done.3, bf16[256,256]{1,0:T(8,128)(2,1)S(1)} %copy-done.2, bf16[256,256]{1,0:T(8,128)(2,1)S(1)} %copy-done.1), custom_call_target="tpu_custom_call" | custom-call | tf_op jit(solution)/shard_map/pallas_call | solution.py:164
  125.7 0.0 copy-start.8
  125.8 0.0 copy-start.7
  125.8 0.0 copy-start.5
  125.8 0.0 copy-start.6
  125.8 97.8 %all_to_all.11.own_ref = bf16[8,32,2,32,128]{4,3,2,1,0:T(8,128)(2,1)} all-to-all(bf16[8,32,2,32,128]{4,3,2,1,0:T(8,128)(2,1)S(1)} %bitcast.8), channel_id=1, replica_groups=mesh['grp'=2,'chan'=2,'tm'=4,'pol'=2] {'chan','tm'}, dimensions={0} | all-to-all | bytes 8388608 | tf_op jit(solution)/shard_map/all_to_all | solution.py:307
  223.6 0.0 collective-permute-start
  223.6 0.0 copy-done.8
  223.6 0.2 reduce-window.8
  223.8 0.1 fusion.1
  223.9 0.0 copy-done.7
  223.9 0.1 multiply_reduce_fusion
  224.0 0.1 convert_element_type.24.weight_ref
  224.1 0.0 copy-done.5
  224.1 0.0 copy-done.6
  224.1 0.1 pad_add_fusion
  224.2 0.1 multiply_reduce_fusion.1
  224.2 0.2 copy.22.rows_ref
  224.5 6.6 %collective-permute-done.other_ref = bf16[8,32,2,32,128]{4,3,2,1,0:T(8,128)(2,1)} collective-permute-done((bf16[8,32,2,32,128]{4,3,2,1,0:T(8,128)(2,1)}, bf16[8,32,2,32,128]{4,3,2,1,0:T(8,128)(2,1)}, u32[]{:S(2)}, u32[]{:S(2)}) %collective-permute-start) | collective-permute-done | bytes 4194336 | tf_op jit(solution)/shard_map/ppermute | solution.py:308
  231.1 24.4 %shard_map.101 = f32[8,32,2,2,64,128]{5,4,3,2,1,0:T(8,128)} custom-call(s32[1]{0:T(128)} %bitcast.place_ref, s32[1024,1]{1,0:T(8,128)S(1)} %copy.22.rows_ref, bf16[8,1,128]{2,1,0:T(2,128)(2,1)S(1)} %convert_element_type.24.weight_ref, bf16[8,32,2,32,128]{4,3,2,1,0:T(8,128)(2,1)} %all_to_all.11.own_ref, ...), custom_call_target="tpu_custom_call" | custom-call | tf_op jit(solution)/shard_map/pallas_call | solution.py:269
  (4 shorter events, 0.0 us)
Async XLA Ops:
  101.7 2.3 copy-start
  101.7 2.3 copy-start.1
  101.7 2.3 copy-start.2
  101.7 2.3 copy-start.3
  101.7 2.3 copy-start.4
  125.7 97.8 %copy-start.8 = (s32[14]{0:T(128)S(1)}, s32[14]{0:T(128)}, u32[]{:S(2)}) copy-start(s32[14]{0:T(128)} %param.14) | copy-start | bytes 172
  125.8 98.1 %copy-start.7 = (s32[14,16]{1,0:T(8,128)S(1)}, s32[14,16]{1,0:T(8,128)}, u32[]{:S(2)}) copy-start(s32[14,16]{1,0:T(8,128)} %param.15) | copy-start | bytes 2692
  125.8 98.3 %copy-start.5 = (s32[14,64]{1,0:T(8,128)S(1)}, s32[14,64]{1,0:T(8,128)}, u32[]{:S(2)}) copy-start(s32[14,64]{1,0:T(8,128)} %param.13) | copy-start | bytes 10756
  125.8 98.3 %copy-start.6 = (s32[14,64]{1,0:T(8,128)S(1)}, s32[14,64]{1,0:T(8,128)}, u32[]{:S(2)}) copy-start(s32[14,64]{1,0:T(8,128)} %param.12) | copy-start | bytes 10756
  223.6 7.5 %collective-permute-start = (bf16[8,32,2,32,128]{4,3,2,1,0:T(8,128)(2,1)}, bf16[8,32,2,32,128]{4,3,2,1,0:T(8,128)(2,1)}, u32[]{:S(2)}, u32[]{:S(2)}) collective-permute-start(bf16[8,32,2,32,128]{4,3,2,1,0:T(8,128)(2,1)} %all_to_all.11.own_ref), channel_id=1, source_target_pairs={{0,1},{1,0},{2,3},{3,2},{4,5},{5,4},{6,7},{7,6},{8,9},{9,8},{10,11... | collective-permute-start | bytes 12582920 | tf_op jit(solution)/shard_map/ppermute | solution.py:308
where the time goes:
time: 256 us; the launch traced here: 255 us
  blocking collectives  197 us (77%)
  Pallas kernels  46.1 us (18%)
  waiting for transfers between devices  6.6 us (3%)
  local copies, waits for them, and re-layouts  5.11 us (2%)
    all_to_all x1, blocking collectives, on_device(): lax.all_to_all(blocks, 'tm', split_axis=1, concat_axis=1, tiled=True)  99.3 us
    all_to_all x1, blocking collectives, on_device(): lax.all_to_all(outgoing, ('chan', 'tm'), split_axis=0, concat_axis=0, til...  97.8 us
    pallas_call x1, Pallas kernels, correlate(): pl.pallas_call(correlate_kernel, grid=(bands // step,), in_specs=[pl.Bloc...  24.4 us
    pallas_call x1, Pallas kernels, local_spectra(): pl.pallas_call(spectra_kernel, grid=(share // block,), in_specs=[pl.Block...  21.7 us
    ppermute x1, waiting for transfers between devices, on_device(): other = lax.ppermute(moved, 'pol', [(0, 1), (1, 0)])  6.6 us
  transfers between devices with their start and end apart: 1, of which 1 were waited for; matrix products, arithmetic and copies ran while one was open for 0% of the time, Pallas kernels for 0%

commit v1 on v0

--- a/solution.py
+++ b/solution.py
@@ -1,3 +1,4 @@
+import functools
 import math
 
 import jax
@@ -13,6 +14,9 @@
 CAP = 8
 
 radix_first = 16
+BLOCK = 16
+LAST = 0
+MESH = pl.DeviceIdType.MESH
 
 
 def fourier(filtered):
@@ -81,13 +85,14 @@
     return result
 
 
-def spectra_kernel(x_ref, taps_ref, cos_ref, sin_ref, high_ref, low_ref, out_ref, held, turned):
-    time_count, block = x_ref.shape[1:3]
+def filter_and_transform(chunk, got, taps_ref, cos_ref, sin_ref, high_ref, low_ref, made, held, turned):
+    time_count, _, _, block, samples_count = got.shape
     taps, length = taps_ref.shape
-    frames = x_ref.shape[3] // length
+    frames = samples_count // length
     spectra_count = time_count * frames
     second = length // radix_first
     depth = AVG * spectra_count
+    owners, _, units = made.shape[:3]
 
     def filter_section(k1, carry):
         at = pl.multiple_of(k1 * second, second)
@@ -96,7 +101,9 @@
             samples = []
             for t in range(spectra_count):
                 place = pl.multiple_of(k1 * second + (t % frames) * length, second)
-                samples.append(x_ref[r, t // frames, :, pl.ds(place, second)].astype(jnp.float32))
+                samples.append(
+                    got[t // frames, chunk, r, :, pl.ds(place, second)].astype(jnp.float32)
+                )
             filtered = []
             for t in range(spectra_count):
                 total = rows[0] * samples[t]
@@ -135,24 +142,156 @@
 
     lax.fori_loop(0, block, transform_station, 0)
 
-    def place_channels(f, carry):
-        at = pl.multiple_of(f * 16, 16)
+    def place_channels(o, carry):
+        at = pl.multiple_of(o * units, units)
         for q in range(2):
             for h in range(radix_first // AVG):
-                part = turned[:, pl.ds(q * second + at, 16), h * depth : (h + 1) * depth]
-                out_ref[pl.ds(at, 16), h, q] = jnp.transpose(part, (1, 0, 2)).astype(jnp.bfloat16)
+                part = turned[:, pl.ds(q * second + at, units), h * depth : (h + 1) * depth]
+                made[o, chunk, :, h, q] = jnp.transpose(part, (1, 0, 2)).astype(jnp.bfloat16)
         return carry
 
-    lax.fori_loop(0, second // 16, place_channels, 0)
-
-
-def local_spectra(blocks, taps_filter):
-    _, time_count, share, samples = blocks.shape
+    lax.fori_loop(0, owners, place_channels, 0)
+
+
+def exchange_kernel(
+    cuts, volt_ref, taps_ref, cos_ref, sin_ref, high_ref, low_ref, *rest
+):
+    (
+        *outs,
+        got,
+        made,
+        held,
+        turned,
+        local_in,
+        send_in,
+        recv_in,
+        local_out,
+        send_out,
+        recv_out,
+        send_pol,
+        recv_pol,
+    ) = rest
+    own, other = outs[:2]
+    later = outs[2] if len(outs) > 2 else None
+    times, chunks, _, block, _ = got.shape
+    owners, _, units = made.shape[:3]
+    inside = own.shape[2]
+    chan, tm, pol = lax.axis_index("chan"), lax.axis_index("tm"), lax.axis_index("pol")
+    me = chan * times + tm
+    pieces = list(zip(cuts[:-1], cuts[1:]))
+
+    def device(k):
+        target = lax.rem(me + k, owners)
+        return {"chan": target // times, "tm": lax.rem(target, times)}, target
+
+    barrier = pltpu.get_barrier_semaphore()
+    for k in range(1, owners):
+        pl.semaphore_signal(barrier, inc=1, device_id=device(k)[0], device_id_type=MESH)
+    pl.semaphore_signal(barrier, inc=1, device_id={"pol": 1 - pol}, device_id_type=MESH)
+    pl.semaphore_wait(barrier, owners)
+
+    def voltages_of(target, chunk):
+        at = pl.multiple_of((target * chunks + chunk) * block, block)
+        return volt_ref.at[:, pl.ds(at, block), :]
+
+    def copy_in(chunk, d):
+        target = lax.rem(tm + d, times)
+        return pltpu.make_async_remote_copy(
+            src_ref=voltages_of(target, chunk),
+            dst_ref=got.at[tm, chunk],
+            send_sem=send_in.at[chunk, d - 1],
+            recv_sem=recv_in.at[chunk, d - 1],
+            device_id={"tm": target},
+            device_id_type=MESH,
+        )
+
+    def keep_in(chunk):
+        return pltpu.make_async_copy(voltages_of(tm, chunk), got.at[tm, chunk], local_in.at[chunk])
+
+    def copy_out(chunk, b, k):
+        to, target = device(k)
+        span = pl.ds(pieces[b][0], pieces[b][1] - pieces[b][0])
+        return pltpu.make_async_remote_copy(
+            src_ref=made.at[target, chunk, span],
+            dst_ref=own.at[me, chunk, span],
+            send_sem=send_out.at[chunk, b, k - 1],
+            recv_sem=recv_out.at[chunk, b, k - 1],
+            device_id=to,
+            device_id_type=MESH,
+        )
+
+    def keep_out(chunk):
+        return pltpu.make_async_copy(
+            made.at[me, chunk, pl.ds(0, inside)], own.at[me, chunk], local_out.at[chunk, 0]
+        )
+
+    def keep_later(chunk):
+        return pltpu.make_async_copy(
+            made.at[:, chunk, pl.ds(inside, units - inside)],
+            later.at[:, chunk],
+            local_out.at[chunk, 1],
+        )
+
+    def copy_pol(chunk, b):
+        span = pl.ds(pieces[b][0], pieces[b][1] - pieces[b][0])
+        return pltpu.make_async_remote_copy(
+            src_ref=own.at[:, chunk, span],
+            dst_ref=other.at[:, chunk, span],
+            send_sem=send_pol.at[chunk, b],
+            recv_sem=recv_pol.at[chunk, b],
+            device_id={"pol": 1 - pol},
+            device_id_type=MESH,
+        )
+
+    for d in range(1, times):
+        copy_in(0, d).start()
+    for chunk in range(chunks):
+        keep_in(chunk).start()
+    for chunk in range(1, chunks):
+        for d in range(1, times):
+            copy_in(chunk - 1, d).wait_send()
+            copy_in(chunk, d).start()
+    for chunk in range(chunks):
+        keep_in(chunk).wait()
+        for d in range(1, times):
+            copy_in(chunk, d).wait_recv()
+        filter_and_transform(
+            chunk, got, taps_ref, cos_ref, sin_ref, high_ref, low_ref, made, held, turned
+        )
+        if chunk == 0:
+            for d in range(1, times):
+                copy_in(chunks - 1, d).wait_send()
+        for b in range(len(pieces)):
+            for k in range(1, owners):
+                copy_out(chunk, b, k).start()
+        keep_out(chunk).start()
+        if later is not None:
+            keep_later(chunk).start()
+    for chunk in range(chunks):
+        keep_out(chunk).wait()
+        if later is not None:
+            keep_later(chunk).wait()
+        for b in range(len(pieces)):
+            for k in range(1, owners):
+                copy_out(chunk, b, k).wait_recv()
+            copy_pol(chunk, b).start()
+    for chunk in range(chunks):
+        for b in range(len(pieces)):
+            for k in range(1, owners):
+                copy_out(chunk, b, k).wait_send()
+            copy_pol(chunk, b).wait()
+
+
+def exchanged_spectra(voltages, taps_filter, owners, times, last):
+    _, stations, samples = voltages.shape
     taps, length = taps_filter.shape
-    spectra_count = time_count * (samples // length)
+    spectra_count = times * (samples // length)
     second = length // radix_first
     depth = AVG * spectra_count
-    block = 16
+    halves = radix_first // AVG
+    chunks = stations // times // BLOCK
+    units = second // owners
+    inside = units - last
     inner = np.arange(second)
     twist = 2.0 * np.pi / length * (np.arange(radix_first)[:, None] * inner[None, :])
     phase = 2.0 * np.pi / second * (inner[:, None] * inner[None, :] % second)
@@ -160,31 +299,42 @@
     matrix = np.block([[c, s], [-s, c]])
     high = matrix.astype(ml_dtypes.bfloat16)
     low = (matrix - high.astype(np.float64)).astype(ml_dtypes.bfloat16)
-    whole = lambda shape: pl.BlockSpec(shape, lambda i: (0, 0))
+    cuts = sorted({0, inside // 3, inside * 2 // 3, inside})
+    pieces = len(cuts) - 1
+    shape = lambda count: jax.ShapeDtypeStruct(
+        (owners, chunks, count, halves, 2, BLOCK, depth), jnp.bfloat16
+    )
+    outs = [shape(inside)] * 2 + ([shape(last)] if last else [])
+    vmem = pl.BlockSpec(memory_space=pltpu.VMEM)
+    anywhere = pl.BlockSpec(memory_space=pl.ANY)
+    dma = pltpu.SemaphoreType.DMA
     return pl.pallas_call(
-        spectra_kernel,
-        grid=(share // block,),
-        in_specs=[
-            pl.BlockSpec((2, time_count, block, samples), lambda i: (0, 0, i, 0)),
-            whole((taps, length)),
-            whole((radix_first, second)),
-            whole((radix_first, second)),
-            whole((2 * second, 2 * second)),
-            whole((2 * second, 2 * second)),
+        functools.partial(exchange_kernel, cuts),
+        in_specs=[anywhere] + [vmem] * 5,
+        out_specs=[anywhere] * len(outs),
+        out_shape=outs,
+        scratch_shapes=[
+            pltpu.VMEM((times, chunks, 2, BLOCK, samples), jnp.bfloat16),
+            pltpu.VMEM((owners, chunks, units, halves, 2, BLOCK, depth), jnp.bfloat16),
+            pltpu.VMEM((2, BLOCK, spectra_count, length), jnp.float32),
+            pltpu.VMEM((BLOCK, 2 * second, radix_first * spectra_count), jnp.float32),
+            dma((chunks,)),
+            dma((chunks, times - 1)),
+            dma((chunks, times - 1)),
+            dma((chunks, 2)),
+            dma((chunks, pieces, owners - 1)),
+            dma((chunks, pieces, owners - 1)),
+            dma((chunks, pieces)),
+            dma((chunks, pieces)),
         ],
-        out_specs=pl.BlockSpec(
-            (second, radix_first // AVG, 2, block, depth), lambda i: (0, 0, 0, i, 0)
+        cost_estimate=pl.CostEstimate(
+            flops=16 * 10**9, bytes_accessed=32 * 2**20, transcendentals=0
         ),
-        out_shape=jax.ShapeDtypeStruct(
-            (second, radix_first // AVG, 2, share, depth), jnp.bfloat16
+        compiler_params=pltpu.CompilerParams(
+            vmem_limit_bytes=40 * 2**20, collective_id=0, has_side_effects=True
         ),
-        scratch_shapes=[
-            pltpu.VMEM((2, block, spectra_count, length), jnp.float32),
-            pltpu.VMEM((block, 2 * second, radix_first * spectra_count), jnp.float32),
-        ],
-        compiler_params=pltpu.CompilerParams(vmem_limit_bytes=48 * 2**20),
     )(
-        blocks,
+        voltages,
         taps_filter,
         np.cos(twist).astype(np.float32),
         np.sin(twist).astype(np.float32),
@@ -216,9 +366,10 @@
     )
 
 
-def correlate_kernel(place_ref, rows_ref, weight_ref, own_ref, other_ref, out_ref, pick, source):
-    sources, bands, parts, part_stations, depth = own_ref.shape
-    stations = sources * part_stations
+def correlate_kernel(place_ref, rows_ref, weight_ref, own_ref, other_ref, *rest):
+    out_ref, pick, source = rest[-3:]
+    sources, chunks, step, halves, parts, block, depth = own_ref.shape
+    stations = sources * chunks * block
     capacity = out_ref.shape[0]
     width = out_ref.shape[4]
 
@@ -227,11 +378,15 @@
         columns = lax.broadcasted_iota(jnp.int32, pick.shape, 1)
         pick[...] = jnp.where(rows_ref[...] == columns, 1.0, 0.0).astype(jnp.bfloat16)
 
-    for band in range(bands):
+    for band in range(step * halves):
         for ref, polarisation in ((own_ref, place_ref[0]), (other_ref, 1 - place_ref[0])):
             at = pl.multiple_of(polarisation * (2 * depth), depth)
             source[band, :, pl.ds(at, 2 * depth)] = jnp.concatenate(
-                [ref[:, band, r].reshape(stations, depth) for r in range(2)], axis=-1
+                [
+                    ref[:, :, band // halves, band % halves, r].reshape(stations, depth)
+                    for r in range(2)
+                ],
+                axis=-1,
             )
         picked = jnp.dot(pick[...], source[band], preferred_element_type=jnp.float32).astype(
             jnp.bfloat16
@@ -262,30 +417,46 @@
             out_ref[slot, band] = result.reshape(2, 2, width, 2 * width)
 
 
-def correlate(place, own, other, rows, weight):
-    sources, bands, parts, part_stations, depth = own.shape
+def correlate(place, own, other, rows, weight, total_bands, first, earlier):
+    sources, chunks, units, halves, parts, block, depth = own.shape
     width = rows.shape[1] // 2
-    step = 2 if bands % 2 == 0 and bands > 2 else 1
+    step = halves
+    given = [] if earlier is None else [earlier]
+    piece = pl.BlockSpec(
+        (sources, chunks, 1, halves, parts, block, depth), lambda g: (0, 0, g, 0, 0, 0, 0)
+    )
     return pl.pallas_call(
         correlate_kernel,
-        grid=(bands // step,),
+        grid=(units,),
         in_specs=[
             pl.BlockSpec(memory_space=pltpu.SMEM),
             pl.BlockSpec((CAP * 2 * width, 1), lambda g: (0, 0)),
             pl.BlockSpec((CAP, 1, depth), lambda g: (0, 0, 0)),
-            pl.BlockSpec((sources, step, parts, part_stations, depth), lambda g: (0, g, 0, 0, 0)),
-            pl.BlockSpec((sources, step, parts, part_stations, depth), lambda g: (0, g, 0, 0, 0)),
+            piece,
+            piece,
+        ]
+        + [pl.BlockSpec(memory_space=pl.ANY)] * len(given),
+        out_specs=pl.BlockSpec(
+            (CAP, step, 2, 2, width, 2 * width), lambda g: (0, g + first, 0, 0, 0, 0)
+        ),
+        out_shape=jax.ShapeDtypeStruct((CAP, total_bands, 2, 2, width, 2 * width), jnp.float32),
+        scratch_shapes=[
+            pltpu.VMEM((CAP * 2 * width, sources * chunks * block), jnp.bfloat16),
+            pltpu.VMEM((step, sources * chunks * block, 4 * depth), jnp.bfloat16),
         ],
-        out_specs=pl.BlockSpec(
-            (CAP, step, 2, 2, width, 2 * width), lambda g: (0, g, 0, 0, 0, 0)
+        input_output_aliases={5: 0} if given else {},
+        cost_estimate=pl.CostEstimate(
+            flops=units * 8 * 10**8, bytes_accessed=units * 2**21, transcendentals=0
         ),
-        out_shape=jax.ShapeDtypeStruct((CAP, bands, 2, 2, width, 2 * width), jnp.float32),
-        scratch_shapes=[
-            pltpu.VMEM((CAP * 2 * width, sources * part_stations), jnp.bfloat16),
-            pltpu.VMEM((step, sources * part_stations, 4 * depth), jnp.bfloat16),
-        ],
         compiler_params=pltpu.CompilerParams(vmem_limit_bytes=48 * 2**20),
-    )(place, rows.reshape(CAP * 2 * width, 1), weight.astype(jnp.bfloat16), own, other)
+    )(
+        place,
+        rows.reshape(CAP * 2 * width, 1),
+        weight.astype(jnp.bfloat16),
+        own,
+        other,
+        *given,
+    )
 
 
 def on_device(voltages, taps_filter, tile_a, tile_b, tile_owner, tile_flags):
@@ -296,16 +467,9 @@
     time_count = lax.axis_size("tm")
     spectra_count = time_count * frames
     share = stations // time_count
-
-    blocks = voltages.reshape(2, time_count, share, frames * length)
-    blocks = lax.all_to_all(blocks, "tm", split_axis=1, concat_axis=1, tiled=True)
-    spectra = (local_spectra if share % 16 == 0 else plain_spectra)(blocks, taps_filter)
-
     owners = chan_count * time_count
     bands = length // (owners * AVG)
-    outgoing = spectra.reshape(owners, bands, 2, share, AVG * spectra_count)
-    moved = lax.all_to_all(outgoing, ("chan", "tm"), split_axis=0, concat_axis=0, tiled=True)
-    other = lax.ppermute(moved, "pol", [(0, 1), (1, 0)])
+    halves = radix_first // AVG
 
     position = lax.axis_index("pol")
     held = tile_owner == position
@@ -317,7 +481,34 @@
     rows = jnp.sum(chosen[:, :, None] * pairs[None], axis=1)[:, :, None]
     flags = jnp.sum(chosen[:, :, None] * tile_flags[None], axis=1)
     weight = jnp.tile(flags.astype(jnp.float32), (1, AVG))[:, None, :]
-    return correlate(position.reshape(1).astype(jnp.int32), moved, other, rows, weight)
+    place = position.reshape(1).astype(jnp.int32)
+    swap = [(0, 1), (1, 0)]
+
+    if share % BLOCK:
+        blocks = voltages.reshape(2, time_count, share, frames * length)
+        blocks = lax.all_to_all(blocks, "tm", split_axis=1, concat_axis=1, tiled=True)
+        spectra = plain_spectra(blocks, taps_filter)
+        outgoing = spectra.reshape(
+            owners, 1, bands // halves, halves, 2, share, AVG * spectra_count
+        )
+        moved = lax.all_to_all(outgoing, ("chan", "tm"), split_axis=0, concat_axis=0, tiled=True)
+        other = lax.ppermute(moved, "pol", swap)
+        return correlate(place, moved, other, rows, weight, bands, 0, None)
+
+    units = bands // halves
+    last = LAST
+    own, other, *later = exchanged_spectra(voltages[:, 0], taps_filter, owners, time_count, last)
+    if last:
+        own_last = lax.all_to_all(
+            later[0], ("chan", "tm"), split_axis=0, concat_axis=0, tiled=True
+        )
+        other_last = lax.ppermute(own_last, "pol", swap)
+    visibility = correlate(place, own, other, rows, weight, bands, 0, None)
+    if last:
+        visibility = correlate(
+            place, own_last, other_last, rows, weight, bands, units - last, visibility
+        )
+    return visibility
 
 
 def solution(mesh):

time: 256 us -> 224 us (0.88)
  blocking collectives: 197 us -> 0 us
  Pallas kernels: 46.1 us -> 212 us
  waiting for transfers between devices: 6.6 us -> 0 us
  local copies, waits for them, and re-layouts: 5.11 us -> 8.54 us
    all_to_all x2 -> x0, blocking collectives: 197 us -> none  [the longest x1 99.3 us: on_device(): lax.all_to_all(blocks, 'tm', split_axis=1, concat_axis=1, tiled=True)]
    pallas_call x2, Pallas kernels: 46.1 us -> 212 us  [the longest x1 189 us: exchanged_spectra(): pl.pallas_call(functools.partial(exchange_kernel, cuts), in_specs=[anywhe...]
    unnamed x18 -> x14, local copies, waits for them, and re-layouts: 0.05 us -> 8.22 us
    ppermute x1 -> x0, waiting for transfers between devices: 6.6 us -> none  [on_device(): other = lax.ppermute(moved, 'pol', [(0, 1), (1, 0)])]
  transfers between devices with their start and end apart: 1 -> 0, of which waited for: 1 -> 0; matrix products, arithmetic and copies ran while one was open for 0% -> 0% of each run, Pallas kernels for 0% -> 0%
where the time goes in v1:
time: 224 us
  Pallas kernels  212 us (95%)
  local copies, waits for them, and re-layouts  8.54 us (4%)
  other arithmetic  2.59 us (1%)
    pallas_call x1, Pallas kernels, exchanged_spectra(): pl.pallas_call(functools.partial(exchange_kernel, cuts), in_specs=[anywhe...  189 us
    pallas_call x1, Pallas kernels, correlate(): pl.pallas_call(correlate_kernel, grid=(units,), in_specs=[pl.BlockSpec(me...  23.6 us
    unnamed x14, local copies, waits for them, and re-layouts  8.22 us

profile of v1, /device:TPU:0, one launch (start us, length us, event | category | flops | bytes accessed | tf_op | source)
XLA Modules:
  0.0 223.5 jit_solution(11497625434371263294)
XLA Ops:
  0.0 0.7 convert_bitcast_fusion
  0.7 0.2 reduce-window.8
  0.9 0.1 fusion.1
  0.9 0.8 multiply_reduce_fusion
  1.7 0.8 pad_add_fusion
  2.5 0.1 multiply_reduce_fusion.1
  2.6 0.1 convert_element_type.24.weight_ref
  2.7 0.2 copy.13.rows_ref
  2.9 0.0 copy-start
  3.0 2.2 copy-done
  5.1 0.0 copy-start.1
  5.1 0.9 copy-done.1
  6.0 0.0 copy-start.2
  6.0 0.9 copy-done.2
  6.9 0.0 copy-start.3
  6.9 0.9 copy-done.3
  7.9 0.0 copy-start.4
  7.9 0.7 copy-done.4
  8.5 0.0 copy-start.5
  8.6 0.7 copy-done.5
  9.2 188.7 %shard_map.100 = (bf16[8,2,16,2,2,16,128]{6,5,4,3,2,1,0:T(8,128)(2,1)S(1)}, bf16[8,2,16,2,2,16,128]{6,5,4,3,2,1,0:T(8,128)(2,1)S(1)}) custom-call(bf16[2,128,8192]{2,1,0:T(8,128)(2,1)S(1)} %bitcast.7, f32[16,2048]{1,0:T(8,128)S(1)} %copy-done.1, f32[16,128]{1,0:T(8,128)S(1)} %copy-done.5, f32[16,128]{1,0:T(8,128)S(1)} %copy-done.4, ...), custom_call_target="tpu_custom_call" | custom-call | flops 16000000000 | bytes 33554432 | tf_op jit(solution)/shard_map/pallas_call | solution.py:311
  198.0 0.0 copy-start.6
  198.0 1.9 copy-done.6
  199.9 23.6 %shard_map.101 = f32[8,32,2,2,64,128]{5,4,3,2,1,0:T(8,128)} custom-call(s32[1]{0:T(128)} %bitcast.place_ref, s32[1024,1]{1,0:T(8,128)S(1)} %copy.13.rows_ref, bf16[8,1,128]{2,1,0:T(2,128)(2,1)S(1)} %convert_element_type.24.weight_ref, bf16[8,2,16,2,2,16,128]{6,5,4,3,2,1,0:T(8,128)(2,1)S(1)} %get-tuple-element.7.own_ref, ...), custom_call_target="tpu_custom_call" | custom-call | flops 12800000000 | bytes 33554432 | tf_op jit(solution)/shard_map/pallas_call | solution.py:428
  (3 shorter events, 0.0 us)
Async XLA Ops:
  2.9 2.2 copy-start
  5.1 0.9 copy-start.1
  6.0 0.9 copy-start.2
  6.9 0.9 copy-start.3
  7.9 0.7 copy-start.4
  8.5 0.7 copy-start.5
  198.0 1.9 copy-start.6

commit v2 on v1

--- a/solution.py
+++ b/solution.py
@@ -15,7 +15,9 @@
 
 radix_first = 16
 BLOCK = 16
-LAST = 0
+LAST = 4
+PIECES = 7
+WINDOW = 2
 MESH = pl.DeviceIdType.MESH
 
 
@@ -153,15 +155,113 @@
     lax.fori_loop(0, owners, place_channels, 0)
 
 
-def exchange_kernel(
-    cuts, volt_ref, taps_ref, cos_ref, sin_ref, high_ref, low_ref, *rest
-):
+def choose_tiles(tile_a_ref, tile_b_ref, owner_ref, flags_ref, pick, weight_ref, mine):
+    tiles, width = tile_a_ref.shape
+    capacity, _, depth = weight_ref.shape
+    stations = pick.shape[1]
+    held = jnp.where(owner_ref[...] == mine, 1.0, 0.0)
+    at = lax.broadcasted_iota(jnp.int32, (tiles, tiles), 0)
+    before = lax.broadcasted_iota(jnp.int32, (tiles, tiles), 1)
+    held = jnp.broadcast_to(held, (tiles, tiles))
+    count = jnp.sum(jnp.where(before <= at, held, 0.0), axis=1, keepdims=True)
+    own = jnp.sum(jnp.where(before == at, held, 0.0), axis=1, keepdims=True)
+    place = jnp.where(own > 0.5, count - 1.0, -1.0)
+    pairs = jnp.concatenate([tile_a_ref[...], tile_b_ref[...]], axis=1).astype(jnp.float32)
+    flags = jnp.concatenate(
+        [flags_ref[...]] * (depth // flags_ref.shape[1]), axis=1
+    ).astype(jnp.float32)
+    column = lax.broadcasted_iota(jnp.int32, (2 * width, stations), 1).astype(jnp.float32)
+    for slot in range(capacity):
+        chosen = jnp.where(place == float(slot), 1.0, 0.0)
+        rows = jnp.sum(chosen * pairs, axis=0, keepdims=True)
+        rows = jnp.transpose(jnp.broadcast_to(rows, (2 * width, 2 * width)), (1, 0))
+        rows = jnp.concatenate([rows] * (stations // (2 * width)), axis=1)
+        pick[slot * 2 * width : (slot + 1) * 2 * width, :] = jnp.where(
+            rows == column, 1.0, 0.0
+        ).astype(jnp.bfloat16)
+        weight = jnp.sum(chosen * flags, axis=0, keepdims=True) * (1.0 / depth)
+        weight_ref[slot] = weight.astype(jnp.bfloat16)
+
+
+def correlate_band(first, second, pick, source, weight_ref, out_ref, band):
+    depth = weight_ref.shape[2]
+    capacity = out_ref.shape[0]
+    width = out_ref.shape[4]
+    for at, data in enumerate(first + second):
+        source[:, at * depth : (at + 1) * depth] = data
+    picked = jnp.dot(pick[...], source[...], preferred_element_type=jnp.float32).astype(
+        jnp.bfloat16
+    )
+    for slot in range(capacity):
+        at = 2 * width * slot
+        weight = weight_ref[slot]
+        left = [picked[at : at + width, i * depth : (i + 1) * depth] * weight for i in range(4)]
+        other = picked[at + width : at + 2 * width]
+        left_rows = jnp.concatenate(
+            [
+                jnp.concatenate([left[0], left[1]], axis=-1),
+                jnp.concatenate([left[2], left[3]], axis=-1),
+                jnp.concatenate([left[1], -left[0]], axis=-1),
+                jnp.concatenate([left[3], -left[2]], axis=-1),
+            ],
+            axis=0,
+        )
+        right_rows = jnp.concatenate([other[:, : 2 * depth], other[:, 2 * depth :]], axis=0)
+        result = lax.dot_general(
+            left_rows, right_rows, (((1,), (1,)), ((), ())), preferred_element_type=jnp.float32
+        )
+        out_ref[slot, band] = result.reshape(2, 2, width, 2 * width)
+
+
+def correlate_unit(unit, own, other, flip, pick, source, weight_ref, out_ref, first_unit=0):
+    sources, chunks, _, halves, parts, block, depth = own.shape
+    stations = sources * chunks * block
+    for half in range(halves):
+        mine = [own[:, :, unit, half, r].reshape(stations, depth) for r in range(parts)]
+        theirs = [other[:, :, unit, half, r].reshape(stations, depth) for r in range(parts)]
+        first = [jnp.where(flip > 0, t, m) for m, t in zip(mine, theirs)]
+        second = [jnp.where(flip > 0, m, t) for m, t in zip(mine, theirs)]
+        band = (unit - first_unit) * halves + half
+        correlate_band(first, second, pick, source.at[half], weight_ref, out_ref, band)
+
+
+def exchange_kernel(cuts, *refs):
     (
-        *outs,
+        volt_ref,
+        taps_any,
+        cos_any,
+        sin_any,
+        high_any,
+        low_any,
+        tile_a_any,
+        tile_b_any,
+        owner_any,
+        flags_any,
+        own_last,
+        other_last,
+        pick,
+        weight_ref,
+        *refs,
+    ) = refs
+    kept, refs = refs[: len(cuts) - 2], refs[len(cuts) - 2 :]
+    (
         got,
         made,
         held,
         turned,
+        own,
+        other,
+        source,
+        taps_ref,
+        cos_ref,
+        sin_ref,
+        high_ref,
+        low_ref,
+        tile_a_ref,
+        tile_b_ref,
+        owner_ref,
+        flags_ref,
+        constant_sem,
         local_in,
         send_in,
         recv_in,
@@ -170,15 +270,14 @@
         recv_out,
         send_pol,
         recv_pol,
-    ) = rest
-    own, other = outs[:2]
-    later = outs[2] if len(outs) > 2 else None
+    ) = refs
     times, chunks, _, block, _ = got.shape
     owners, _, units = made.shape[:3]
     inside = own.shape[2]
     chan, tm, pol = lax.axis_index("chan"), lax.axis_index("tm"), lax.axis_index("pol")
     me = chan * times + tm
     pieces = list(zip(cuts[:-1], cuts[1:]))
+    count = len(pieces)
 
     def device(k):
         target = lax.rem(me + k, owners)
@@ -208,45 +307,74 @@
     def keep_in(chunk):
         return pltpu.make_async_copy(voltages_of(tm, chunk), got.at[tm, chunk], local_in.at[chunk])
 
+    constants = [
+        pltpu.make_async_copy(source_ref, held_ref, constant_sem.at[i])
+        for i, (source_ref, held_ref) in enumerate(
+            (
+                (taps_any, taps_ref),
+                (cos_any, cos_ref),
+                (sin_any, sin_ref),
+                (high_any, high_ref),
+                (low_any, low_ref),
+                (tile_a_any, tile_a_ref),
+                (tile_b_any, tile_b_ref),
+                (owner_any, owner_ref),
+                (flags_any, flags_ref),
+            )
+        )
+    ]
+
+    def landing(refs, b):
+        start, end = pieces[b]
+        if start >= inside:
+            return refs[1], pl.ds(start - inside, end - start)
+        return refs[0], pl.ds(start, end - start)
+
     def copy_out(chunk, b, k):
         to, target = device(k)
-        span = pl.ds(pieces[b][0], pieces[b][1] - pieces[b][0])
+        ref, span = landing((own, own_last), b)
         return pltpu.make_async_remote_copy(
-            src_ref=made.at[target, chunk, span],
-            dst_ref=own.at[me, chunk, span],
+            src_ref=made.at[target, chunk, pl.ds(pieces[b][0], pieces[b][1] - pieces[b][0])],
+            dst_ref=ref.at[me, chunk, span],
             send_sem=send_out.at[chunk, b, k - 1],
             recv_sem=recv_out.at[chunk, b, k - 1],
             device_id=to,
             device_id_type=MESH,
         )
 
-    def keep_out(chunk):
+    def keep_out(chunk, b):
+        ref, span = landing((own, own_last), b)
         return pltpu.make_async_copy(
-            made.at[me, chunk, pl.ds(0, inside)], own.at[me, chunk], local_out.at[chunk, 0]
-        )
-
-    def keep_later(chunk):
-        return pltpu.make_async_copy(
-            made.at[:, chunk, pl.ds(inside, units - inside)],
-            later.at[:, chunk],
-            local_out.at[chunk, 1],
-        )
-
-    def copy_pol(chunk, b):
-        span = pl.ds(pieces[b][0], pieces[b][1] - pieces[b][0])
+            made.at[me, chunk, pl.ds(pieces[b][0], pieces[b][1] - pieces[b][0])],
+            ref.at[me, chunk, span],
+            local_out.at[chunk, b],
+        )
+
+    def copy_pol(b):
+        ref, span = landing((own, own_last), b)
+        target, _ = landing((other, other_last), b)
         return pltpu.make_async_remote_copy(
-            src_ref=own.at[:, chunk, span],
-            dst_ref=other.at[:, chunk, span],
-            send_sem=send_pol.at[chunk, b],
-            recv_sem=recv_pol.at[chunk, b],
+            src_ref=ref.at[:, :, span],
+            dst_ref=target.at[:, :, span],
+            send_sem=send_pol.at[b],
+            recv_sem=recv_pol.at[b],
             device_id={"pol": 1 - pol},
             device_id_type=MESH,
         )
+
+    def send(chunk, b):
+        for k in range(1, owners):
+            copy_out(chunk, b, k).start()
 
     for d in range(1, times):
         copy_in(0, d).start()
     for chunk in range(chunks):
         keep_in(chunk).start()
+    for copy in constants:
+        copy.start()
+    for copy in constants:
+        copy.wait()
+    choose_tiles(tile_a_ref, tile_b_ref, owner_ref, flags_ref, pick, weight_ref, pol)
     for chunk in range(1, chunks):
         for d in range(1, times):
             copy_in(chunk - 1, d).wait_send()
@@ -261,28 +389,41 @@
         if chunk == 0:
             for d in range(1, times):
                 copy_in(chunks - 1, d).wait_send()
-        for b in range(len(pieces)):
-            for k in range(1, owners):
-                copy_out(chunk, b, k).start()
-        keep_out(chunk).start()
-        if later is not None:
-            keep_later(chunk).start()
-    for chunk in range(chunks):
-        keep_out(chunk).wait()
-        if later is not None:
-            keep_later(chunk).wait()
-        for b in range(len(pieces)):
+        for b in range(count):
+            keep_out(chunk, b).start()
+            if chunk < chunks - 1 or b < WINDOW:
+                send(chunk, b)
+    for b in range(count):
+        for chunk in range(chunks):
+            keep_out(chunk, b).wait()
             for k in range(1, owners):
                 copy_out(chunk, b, k).wait_recv()
-            copy_pol(chunk, b).start()
-    for chunk in range(chunks):
-        for b in range(len(pieces)):
+        copy_pol(b).start()
+        if b + WINDOW < count:
             for k in range(1, owners):
-                copy_out(chunk, b, k).wait_send()
-            copy_pol(chunk, b).wait()
-
-
-def exchanged_spectra(voltages, taps_filter, owners, times, last):
+                copy_out(chunks - 1, b, k).wait_send()
+            send(chunks - 1, b + WINDOW)
+        if pieces[b][1] <= inside:
+            copy_pol(b).wait_recv()
+
+            def one_unit(unit, carry, b=b):
+                correlate_unit(
+                    unit, own, other, pol, pick, source, weight_ref, kept[b], pieces[b][0]
+                )
+                return carry
+
+            lax.fori_loop(pieces[b][0], pieces[b][1], one_unit, 0)
+    for b in range(count):
+        for chunk in range(chunks):
+            if chunk < chunks - 1 or b + WINDOW >= count:
+                for k in range(1, owners):
+                    copy_out(chunk, b, k).wait_send()
+        copy_pol(b).wait_send()
+        if pieces[b][0] >= inside:
+            copy_pol(b).wait_recv()
+
+
+def exchange(voltages, taps_filter, tile_a, tile_b, tile_owner, tile_flags, owners, times):
     _, stations, samples = voltages.shape
     taps, length = taps_filter.shape
     spectra_count = times * (samples // length)
@@ -291,7 +432,8 @@
     halves = radix_first // AVG
     chunks = stations // times // BLOCK
     units = second // owners
-    inside = units - last
+    inside = units - LAST
+    tiles, width = tile_a.shape
     inner = np.arange(second)
     twist = 2.0 * np.pi / length * (np.arange(radix_first)[:, None] * inner[None, :])
     phase = 2.0 * np.pi / second * (inner[:, None] * inner[None, :] % second)
@@ -299,48 +441,118 @@
     matrix = np.block([[c, s], [-s, c]])
     high = matrix.astype(ml_dtypes.bfloat16)
     low = (matrix - high.astype(np.float64)).astype(ml_dtypes.bfloat16)
-    cuts = sorted({0, inside // 3, inside * 2 // 3, inside})
-    pieces = len(cuts) - 1
-    shape = lambda count: jax.ShapeDtypeStruct(
-        (owners, chunks, count, halves, 2, BLOCK, depth), jnp.bfloat16
-    )
-    outs = [shape(inside)] * 2 + ([shape(last)] if last else [])
+    cuts = [inside * i // (PIECES - 1) for i in range(PIECES)] + [units]
+    shape = lambda count: (owners, chunks, count, halves, 2, BLOCK, depth)
     vmem = pl.BlockSpec(memory_space=pltpu.VMEM)
     anywhere = pl.BlockSpec(memory_space=pl.ANY)
     dma = pltpu.SemaphoreType.DMA
+    far = lambda value: pltpu.with_memory_space_constraint(jnp.asarray(value), pltpu.HBM)
     return pl.pallas_call(
         functools.partial(exchange_kernel, cuts),
-        in_specs=[anywhere] + [vmem] * 5,
-        out_specs=[anywhere] * len(outs),
-        out_shape=outs,
+        in_specs=[pl.BlockSpec(memory_space=pltpu.HBM)] * 10,
+        out_specs=[anywhere] * 2 + [vmem] * (1 + PIECES),
+        out_shape=[
+            jax.ShapeDtypeStruct(shape(LAST), jnp.bfloat16),
+            jax.ShapeDtypeStruct(shape(LAST), jnp.bfloat16),
+            jax.ShapeDtypeStruct((CAP * 2 * width, owners * chunks * BLOCK), jnp.bfloat16),
+            jax.ShapeDtypeStruct((CAP, 1, depth), jnp.bfloat16),
+        ]
+        + [
+            jax.ShapeDtypeStruct((CAP, (end - start) * halves, 2, 2, width, 2 * width), jnp.float32)
+            for start, end in zip(cuts[:-2], cuts[1:-1])
+        ],
         scratch_shapes=[
             pltpu.VMEM((times, chunks, 2, BLOCK, samples), jnp.bfloat16),
-            pltpu.VMEM((owners, chunks, units, halves, 2, BLOCK, depth), jnp.bfloat16),
+            pltpu.VMEM(shape(units), jnp.bfloat16),
             pltpu.VMEM((2, BLOCK, spectra_count, length), jnp.float32),
             pltpu.VMEM((BLOCK, 2 * second, radix_first * spectra_count), jnp.float32),
+            pltpu.VMEM(shape(inside), jnp.bfloat16),
+            pltpu.VMEM(shape(inside), jnp.bfloat16),
+            pltpu.VMEM((halves, owners * chunks * BLOCK, 4 * depth), jnp.bfloat16),
+            pltpu.VMEM((taps, length), jnp.float32),
+            pltpu.VMEM((radix_first, second), jnp.float32),
+            pltpu.VMEM((radix_first, second), jnp.float32),
+            pltpu.VMEM((2 * second, 2 * second), jnp.bfloat16),
+            pltpu.VMEM((2 * second, 2 * second), jnp.bfloat16),
+            pltpu.VMEM((tiles, width), jnp.int32),
+            pltpu.VMEM((tiles, width), jnp.int32),
+            pltpu.VMEM((1, tiles), jnp.int32),
+            pltpu.VMEM(tile_flags.shape, jnp.int32),
+            dma((9,)),
             dma((chunks,)),
             dma((chunks, times - 1)),
             dma((chunks, times - 1)),
-            dma((chunks, 2)),
-            dma((chunks, pieces, owners - 1)),
-            dma((chunks, pieces, owners - 1)),
-            dma((chunks, pieces)),
-            dma((chunks, pieces)),
+            dma((chunks, PIECES)),
+            dma((chunks, PIECES, owners - 1)),
+            dma((chunks, PIECES, owners - 1)),
+            dma((PIECES,)),
+            dma((PIECES,)),
         ],
         cost_estimate=pl.CostEstimate(
             flops=16 * 10**9, bytes_accessed=32 * 2**20, transcendentals=0
         ),
         compiler_params=pltpu.CompilerParams(
-            vmem_limit_bytes=40 * 2**20, collective_id=0, has_side_effects=True
+            vmem_limit_bytes=24 * 2**20, collective_id=0, has_side_effects=True
         ),
     )(
         voltages,
-        taps_filter,
-        np.cos(twist).astype(np.float32),
-        np.sin(twist).astype(np.float32),
-        high,
-        low,
-    )
+        far(taps_filter),
+        far(np.cos(twist).astype(np.float32)),
+        far(np.sin(twist).astype(np.float32)),
+        far(high),
+        far(low),
+        far(tile_a),
+        far(tile_b),
+        far(tile_owner.reshape(1, tiles)),
+        far(tile_flags),
+    )
+
+
+def finish_kernel(own, other, pick, weight_ref, *refs):
+    *kept, out_ref, source, block, kept_sem, block_sem = refs
+    units, halves = own.shape[2:4]
+    pol = lax.axis_index("pol")
+    copies, inside = [], 0
+    for i, vis in enumerate(kept):
+        bands = vis.shape[1]
+        copies.append(
+            pltpu.make_async_copy(vis, out_ref.at[:, pl.ds(inside, bands)], kept_sem.at[i])
+        )
+        inside += bands
+    for copy in copies:
+        copy.start()
+    for unit in range(units):
+        correlate_unit(unit, own, other, pol, pick, source, weight_ref, block)
+        copy = pltpu.make_async_copy(
+            block.at[:, pl.ds(unit * halves, halves)],
+            out_ref.at[:, pl.ds(inside + unit * halves, halves)],
+            block_sem.at[unit],
+        )
+        copy.start()
+        copies.append(copy)
+    for copy in copies:
+        copy.wait()
+
+
+def finish(own, other, pick, weight, *kept):
+    capacity = kept[0].shape[0]
+    inside = sum(vis.shape[1] for vis in kept)
+    sources, chunks, units, halves, _, block, depth = own.shape
+    rest = kept[0].shape[2:]
+    vmem = pl.BlockSpec(memory_space=pltpu.VMEM)
+    return pl.pallas_call(
+        finish_kernel,
+        in_specs=[vmem] * (4 + len(kept)),
+        out_specs=pl.BlockSpec(memory_space=pl.ANY),
+        out_shape=jax.ShapeDtypeStruct((capacity, inside + units * halves) + rest, jnp.float32),
+        scratch_shapes=[
+            pltpu.VMEM((halves, sources * chunks * block, 4 * depth), jnp.bfloat16),
+            pltpu.VMEM((capacity, units * halves) + rest, jnp.float32),
+            pltpu.SemaphoreType.DMA((len(kept),)),
+            pltpu.SemaphoreType.DMA((units,)),
+        ],
+        compiler_params=pltpu.CompilerParams(vmem_limit_bytes=14 * 2**20),
+    )(own, other, pick, weight, *kept)
 
 
 def plain_spectra(blocks, taps_filter):
@@ -471,6 +683,19 @@
     bands = length // (owners * AVG)
     halves = radix_first // AVG
 
+    if share % BLOCK == 0:
+        results = exchange(
+            voltages[:, 0],
+            taps_filter,
+            tile_a,
+            tile_b,
+            tile_owner,
+            tile_flags,
+            owners,
+            time_count,
+        )
+        return finish(*results)
+
     position = lax.axis_index("pol")
     held = tile_owner == position
     rank = jnp.cumsum(held.astype(jnp.int32)) - 1
@@ -484,31 +709,13 @@
     place = position.reshape(1).astype(jnp.int32)
     swap = [(0, 1), (1, 0)]
 
-    if share % BLOCK:
-        blocks = voltages.reshape(2, time_count, share, frames * length)
-        blocks = lax.all_to_all(blocks, "tm", split_axis=1, concat_axis=1, tiled=True)
-        spectra = plain_spectra(blocks, taps_filter)
-        outgoing = spectra.reshape(
-            owners, 1, bands // halves, halves, 2, share, AVG * spectra_count
-        )
-        moved = lax.all_to_all(outgoing, ("chan", "tm"), split_axis=0, concat_axis=0, tiled=True)
-        other = lax.ppermute(moved, "pol", swap)
-        return correlate(place, moved, other, rows, weight, bands, 0, None)
-
-    units = bands // halves
-    last = LAST
-    own, other, *later = exchanged_spectra(voltages[:, 0], taps_filter, owners, time_count, last)
-    if last:
-        own_last = lax.all_to_all(
-            later[0], ("chan", "tm"), split_axis=0, concat_axis=0, tiled=True
-        )
-        other_last = lax.ppermute(own_last, "pol", swap)
-    visibility = correlate(place, own, other, rows, weight, bands, 0, None)
-    if last:
-        visibility = correlate(
-            place, own_last, other_last, rows, weight, bands, units - last, visibility
-        )
-    return visibility
+    blocks = voltages.reshape(2, time_count, share, frames * length)
+    blocks = lax.all_to_all(blocks, "tm", split_axis=1, concat_axis=1, tiled=True)
+    spectra = plain_spectra(blocks, taps_filter)
+    outgoing = spectra.reshape(owners, 1, bands // halves, halves, 2, share, AVG * spectra_count)
+    moved = lax.all_to_all(outgoing, ("chan", "tm"), split_axis=0, concat_axis=0, tiled=True)
+    other = lax.ppermute(moved, "pol", swap)
+    return correlate(place, moved, other, rows, weight, bands, 0, None)
 
 
 def solution(mesh):

time: 224 us -> 203 us (0.906)
  Pallas kernels: 212 us -> 202 us
  local copies, waits for them, and re-layouts: 8.54 us -> 0 us
  other arithmetic: 2.59 us -> 0 us
    pallas_call x2, Pallas kernels: 212 us -> 202 us  [the longest x1 191 us: exchange(): pl.pallas_call(functools.partial(exchange_kernel, cuts), in_specs=[pl.Blo...]
    unnamed x14 -> x0, local copies, waits for them, and re-layouts: 8.22 us -> none
where the time goes in v2:
time: 203 us
  Pallas kernels  202 us (100%)
    pallas_call x1, Pallas kernels, exchange(): pl.pallas_call(functools.partial(exchange_kernel, cuts), in_specs=[pl.Blo...  191 us
    pallas_call x1, Pallas kernels, finish(): pl.pallas_call(finish_kernel, in_specs=[vmem] * (4 + len(kept)), out_spec...  11 us

profile of v2, /device:TPU:0, one launch (start us, length us, event | category | flops | bytes accessed | tf_op | source)
XLA Modules:
  0.0 202.6 jit_solution(11810359691498544710)
XLA Ops:
  0.0 191.4 %shard_map.100 = (bf16[8,2,4,2,2,16,128]{6,5,4,3,2,1,0:T(8,128)(2,1)S(1)}, bf16[8,2,4,2,2,16,128]{6,5,4,3,2,1,0:T(8,128)(2,1)S(1)}, bf16[1024,256]{1,0:T(8,128)(...) custom-call(bf16[2,128,8192]{2,1,0:T(8,128)(2,1)} %bitcast.2, ...), custom_call_target="tpu_custom_call" | custom-call | flops 16000000000 | bytes 33554432 | tf_op jit(solution)/shard_map/pallas_call | solution.py:450
  191.4 11.0 %shard_map.101 = f32[8,32,2,2,64,128]{5,4,3,2,1,0:T(8,128)} custom-call(bf16[8,2,4,2,2,16,128]{6,5,4,3,2,1,0:T(8,128)(2,1)S(1)} %get-tuple-element.15.own, bf16[8,2,4,2,2,16,128]{6,5,4,3,2,1,0:T(8,128)(2,1)S(1)} %get-tuple-element.16.other, bf16[1024,256]{1,0:T(8,128)(2,1)S(1)} %get-tuple-element.17.pick, ...), custom_call_target="tpu_custom_call" | custom-call | tf_op jit(solution)/shard_map/pallas_call | solution.py:543

commit v3 on v2

--- a/solution.py
+++ b/solution.py
@@ -15,9 +15,9 @@
 
 radix_first = 16
 BLOCK = 16
-LAST = 4
-PIECES = 7
-WINDOW = 2
+LAST = 6
+KEEP = 2
+WINDOW = 3
 MESH = pl.DeviceIdType.MESH
 
 
@@ -183,15 +183,12 @@
         weight_ref[slot] = weight.astype(jnp.bfloat16)
 
 
-def correlate_band(first, second, pick, source, weight_ref, out_ref, band):
+def correlate_band(first, second, pick, weight_ref, out_ref, band):
     depth = weight_ref.shape[2]
     capacity = out_ref.shape[0]
     width = out_ref.shape[4]
-    for at, data in enumerate(first + second):
-        source[:, at * depth : (at + 1) * depth] = data
-    picked = jnp.dot(pick[...], source[...], preferred_element_type=jnp.float32).astype(
-        jnp.bfloat16
-    )
+    data = jnp.concatenate(first + second, axis=-1)
+    picked = jnp.dot(pick[...], data, preferred_element_type=jnp.float32).astype(jnp.bfloat16)
     for slot in range(capacity):
         at = 2 * width * slot
         weight = weight_ref[slot]
@@ -213,7 +210,7 @@
         out_ref[slot, band] = result.reshape(2, 2, width, 2 * width)
 
 
-def correlate_unit(unit, own, other, flip, pick, source, weight_ref, out_ref, first_unit=0):
+def correlate_unit(unit, own, other, flip, pick, weight_ref, out_ref, first_unit=0):
     sources, chunks, _, halves, parts, block, depth = own.shape
     stations = sources * chunks * block
     for half in range(halves):
@@ -222,10 +219,10 @@
         first = [jnp.where(flip > 0, t, m) for m, t in zip(mine, theirs)]
         second = [jnp.where(flip > 0, m, t) for m, t in zip(mine, theirs)]
         band = (unit - first_unit) * halves + half
-        correlate_band(first, second, pick, source.at[half], weight_ref, out_ref, band)
-
-
-def exchange_kernel(cuts, *refs):
+        correlate_band(first, second, pick, weight_ref, out_ref, band)
+
+
+def exchange_kernel(early_cuts, late_cuts, *refs):
     (
         volt_ref,
         taps_any,
@@ -243,7 +240,7 @@
         weight_ref,
         *refs,
     ) = refs
-    kept, refs = refs[: len(cuts) - 2], refs[len(cuts) - 2 :]
+    kept, refs = refs[:-24], refs[-24:]
     (
         got,
         made,
@@ -251,7 +248,6 @@
         turned,
         own,
         other,
-        source,
         taps_ref,
         cos_ref,
         sin_ref,
@@ -276,8 +272,10 @@
     inside = own.shape[2]
     chan, tm, pol = lax.axis_index("chan"), lax.axis_index("tm"), lax.axis_index("pol")
     me = chan * times + tm
-    pieces = list(zip(cuts[:-1], cuts[1:]))
-    count = len(pieces)
+    spans = lambda cuts: list(zip(cuts[:-1], cuts[1:]))
+    pieces = [spans(early_cuts)] * (chunks - 1) + [spans(late_cuts)]
+    lately = chunks - 1
+    count = len(pieces[lately])
 
     def device(k):
         target = lax.rem(me + k, owners)
@@ -293,13 +291,13 @@
         at = pl.multiple_of((target * chunks + chunk) * block, block)
         return volt_ref.at[:, pl.ds(at, block), :]
 
-    def copy_in(chunk, d):
+    def copy_in(chunk, r, d):
         target = lax.rem(tm + d, times)
         return pltpu.make_async_remote_copy(
-            src_ref=voltages_of(target, chunk),
-            dst_ref=got.at[tm, chunk],
-            send_sem=send_in.at[chunk, d - 1],
-            recv_sem=recv_in.at[chunk, d - 1],
+            src_ref=voltages_of(target, chunk).at[r],
+            dst_ref=got.at[tm, chunk, r],
+            send_sem=send_in.at[chunk, r, d - 1],
+            recv_sem=recv_in.at[chunk, r, d - 1],
             device_id={"tm": target},
             device_id_type=MESH,
         )
@@ -324,17 +322,18 @@
         )
     ]
 
-    def landing(refs, b):
-        start, end = pieces[b]
+    def landing(refs, piece):
+        start, end = piece
         if start >= inside:
             return refs[1], pl.ds(start - inside, end - start)
         return refs[0], pl.ds(start, end - start)
 
     def copy_out(chunk, b, k):
         to, target = device(k)
-        ref, span = landing((own, own_last), b)
+        start, end = pieces[chunk][b]
+        ref, span = landing((own, own_last), (start, end))
         return pltpu.make_async_remote_copy(
-            src_ref=made.at[target, chunk, pl.ds(pieces[b][0], pieces[b][1] - pieces[b][0])],
+            src_ref=made.at[target, chunk, pl.ds(start, end - start)],
             dst_ref=ref.at[me, chunk, span],
             send_sem=send_out.at[chunk, b, k - 1],
             recv_sem=recv_out.at[chunk, b, k - 1],
@@ -343,16 +342,17 @@
         )
 
     def keep_out(chunk, b):
-        ref, span = landing((own, own_last), b)
+        start, end = pieces[chunk][b]
+        ref, span = landing((own, own_last), (start, end))
         return pltpu.make_async_copy(
-            made.at[me, chunk, pl.ds(pieces[b][0], pieces[b][1] - pieces[b][0])],
+            made.at[me, chunk, pl.ds(start, end - start)],
             ref.at[me, chunk, span],
             local_out.at[chunk, b],
         )
 
     def copy_pol(b):
-        ref, span = landing((own, own_last), b)
-        target, _ = landing((other, other_last), b)
+        ref, span = landing((own, own_last), pieces[lately][b])
+        target, _ = landing((other, other_last), pieces[lately][b])
         return pltpu.make_async_remote_copy(
             src_ref=ref.at[:, :, span],
             dst_ref=target.at[:, :, span],
@@ -366,8 +366,14 @@
         for k in range(1, owners):
             copy_out(chunk, b, k).start()
 
-    for d in range(1, times):
-        copy_in(0, d).start()
+    def await_out(chunk, b):
+        keep_out(chunk, b).wait()
+        for k in range(1, owners):
+            copy_out(chunk, b, k).wait_recv()
+
+    for r in range(2):
+        for d in range(1, times):
+            copy_in(0, r, d).start()
     for chunk in range(chunks):
         keep_in(chunk).start()
     for copy in constants:
@@ -376,50 +382,58 @@
         copy.wait()
     choose_tiles(tile_a_ref, tile_b_ref, owner_ref, flags_ref, pick, weight_ref, pol)
     for chunk in range(1, chunks):
-        for d in range(1, times):
-            copy_in(chunk - 1, d).wait_send()
-            copy_in(chunk, d).start()
+        for r in range(2):
+            for d in range(1, times):
+                copy_in(chunk - 1, r, d).wait_send()
+                copy_in(chunk, r, d).start()
     for chunk in range(chunks):
         keep_in(chunk).wait()
-        for d in range(1, times):
-            copy_in(chunk, d).wait_recv()
+        for r in range(2):
+            for d in range(1, times):
+                copy_in(chunk, r, d).wait_recv()
         filter_and_transform(
             chunk, got, taps_ref, cos_ref, sin_ref, high_ref, low_ref, made, held, turned
         )
-        if chunk == 0:
-            for d in range(1, times):
-                copy_in(chunks - 1, d).wait_send()
-        for b in range(count):
+        for b in range(len(pieces[chunk])):
             keep_out(chunk, b).start()
-            if chunk < chunks - 1 or b < WINDOW:
+            if chunk < lately or b < WINDOW:
                 send(chunk, b)
-    for b in range(count):
-        for chunk in range(chunks):
-            keep_out(chunk, b).wait()
-            for k in range(1, owners):
-                copy_out(chunk, b, k).wait_recv()
+            if chunk == 0 and b == 0:
+                for r in range(2):
+                    for d in range(1, times):
+                        copy_in(lately, r, d).wait_send()
+    for b, (start, end) in enumerate(pieces[lately]):
+        await_out(lately, b)
+        for chunk in range(lately):
+            for early, piece in enumerate(pieces[chunk]):
+                if start <= piece[0] < end:
+                    await_out(chunk, early)
         copy_pol(b).start()
         if b + WINDOW < count:
             for k in range(1, owners):
-                copy_out(chunks - 1, b, k).wait_send()
-            send(chunks - 1, b + WINDOW)
-        if pieces[b][1] <= inside:
+                copy_out(lately, b, k).wait_send()
+            send(lately, b + WINDOW)
+        if end <= inside:
             copy_pol(b).wait_recv()
-
-            def one_unit(unit, carry, b=b):
-                correlate_unit(
-                    unit, own, other, pol, pick, source, weight_ref, kept[b], pieces[b][0]
-                )
-                return carry
-
-            lax.fori_loop(pieces[b][0], pieces[b][1], one_unit, 0)
-    for b in range(count):
-        for chunk in range(chunks):
-            if chunk < chunks - 1 or b + WINDOW >= count:
-                for k in range(1, owners):
-                    copy_out(chunk, b, k).wait_send()
+            for at in range(start // KEEP, end // KEEP):
+
+                def one_unit(unit, carry, at=at):
+                    correlate_unit(
+                        unit, own, other, pol, pick, weight_ref, kept[at], at * KEEP
+                    )
+                    return carry
+
+                lax.fori_loop(at * KEEP, (at + 1) * KEEP, one_unit, 0)
+    for chunk in range(lately):
+        for b in range(len(pieces[chunk])):
+            for k in range(1, owners):
+                copy_out(chunk, b, k).wait_send()
+    for b, (start, _) in enumerate(pieces[lately]):
+        if b + WINDOW >= count:
+            for k in range(1, owners):
+                copy_out(lately, b, k).wait_send()
         copy_pol(b).wait_send()
-        if pieces[b][0] >= inside:
+        if start >= inside:
             copy_pol(b).wait_recv()
 
 
@@ -441,16 +455,18 @@
     matrix = np.block([[c, s], [-s, c]])
     high = matrix.astype(ml_dtypes.bfloat16)
     low = (matrix - high.astype(np.float64)).astype(ml_dtypes.bfloat16)
-    cuts = [inside * i // (PIECES - 1) for i in range(PIECES)] + [units]
+    early = [0, inside, units]
+    late = [0, inside * 2 // 5, inside * 4 // 5, inside, units - 2, units - 1, units]
+    count = max(len(early), len(late)) - 1
     shape = lambda count: (owners, chunks, count, halves, 2, BLOCK, depth)
     vmem = pl.BlockSpec(memory_space=pltpu.VMEM)
     anywhere = pl.BlockSpec(memory_space=pl.ANY)
     dma = pltpu.SemaphoreType.DMA
     far = lambda value: pltpu.with_memory_space_constraint(jnp.asarray(value), pltpu.HBM)
     return pl.pallas_call(
-        functools.partial(exchange_kernel, cuts),
+        functools.partial(exchange_kernel, early, late),
         in_specs=[pl.BlockSpec(memory_space=pltpu.HBM)] * 10,
-        out_specs=[anywhere] * 2 + [vmem] * (1 + PIECES),
+        out_specs=[anywhere] * 2 + [vmem] * (2 + inside // KEEP),
         out_shape=[
             jax.ShapeDtypeStruct(shape(LAST), jnp.bfloat16),
             jax.ShapeDtypeStruct(shape(LAST), jnp.bfloat16),
@@ -458,9 +474,9 @@
             jax.ShapeDtypeStruct((CAP, 1, depth), jnp.bfloat16),
         ]
         + [
-            jax.ShapeDtypeStruct((CAP, (end - start) * halves, 2, 2, width, 2 * width), jnp.float32)
-            for start, end in zip(cuts[:-2], cuts[1:-1])
-        ],
+            jax.ShapeDtypeStruct((CAP, KEEP * halves, 2, 2, width, 2 * width), jnp.float32)
+        ]
+        * (inside // KEEP),
         scratch_shapes=[
             pltpu.VMEM((times, chunks, 2, BLOCK, samples), jnp.bfloat16),
             pltpu.VMEM(shape(units), jnp.bfloat16),
@@ -468,7 +484,6 @@
             pltpu.VMEM((BLOCK, 2 * second, radix_first * spectra_count), jnp.float32),
             pltpu.VMEM(shape(inside), jnp.bfloat16),
             pltpu.VMEM(shape(inside), jnp.bfloat16),
-            pltpu.VMEM((halves, owners * chunks * BLOCK, 4 * depth), jnp.bfloat16),
             pltpu.VMEM((taps, length), jnp.float32),
             pltpu.VMEM((radix_first, second), jnp.float32),
             pltpu.VMEM((radix_first, second), jnp.float32),
@@ -480,13 +495,13 @@
             pltpu.VMEM(tile_flags.shape, jnp.int32),
             dma((9,)),
             dma((chunks,)),
-            dma((chunks, times - 1)),
-            dma((chunks, times - 1)),
-            dma((chunks, PIECES)),
-            dma((chunks, PIECES, owners - 1)),
-            dma((chunks, PIECES, owners - 1)),
-            dma((PIECES,)),
-            dma((PIECES,)),
+            dma((chunks, 2, times - 1)),
+            dma((chunks, 2, times - 1)),
+            dma((chunks, count)),
+            dma((chunks, count, owners - 1)),
+            dma((chunks, count, owners - 1)),
+            dma((count,)),
+            dma((count,)),
         ],
         cost_estimate=pl.CostEstimate(
             flops=16 * 10**9, bytes_accessed=32 * 2**20, transcendentals=0
@@ -495,7 +510,7 @@
             vmem_limit_bytes=24 * 2**20, collective_id=0, has_side_effects=True
         ),
     )(
-        voltages,
+        far(voltages),
         far(taps_filter),
         far(np.cos(twist).astype(np.float32)),
         far(np.sin(twist).astype(np.float32)),
@@ -509,7 +524,7 @@
 
 
 def finish_kernel(own, other, pick, weight_ref, *refs):
-    *kept, out_ref, source, block, kept_sem, block_sem = refs
+    *kept, out_ref, block, kept_sem, block_sem = refs
     units, halves = own.shape[2:4]
     pol = lax.axis_index("pol")
     copies, inside = [], 0
@@ -522,7 +537,7 @@
     for copy in copies:
         copy.start()
     for unit in range(units):
-        correlate_unit(unit, own, other, pol, pick, source, weight_ref, block)
+        correlate_unit(unit, own, other, pol, pick, weight_ref, block)
         copy = pltpu.make_async_copy(
             block.at[:, pl.ds(unit * halves, halves)],
             out_ref.at[:, pl.ds(inside + unit * halves, halves)],
@@ -546,12 +561,11 @@
         out_specs=pl.BlockSpec(memory_space=pl.ANY),
         out_shape=jax.ShapeDtypeStruct((capacity, inside + units * halves) + rest, jnp.float32),
         scratch_shapes=[
-            pltpu.VMEM((halves, sources * chunks * block, 4 * depth), jnp.bfloat16),
             pltpu.VMEM((capacity, units * halves) + rest, jnp.float32),
             pltpu.SemaphoreType.DMA((len(kept),)),
             pltpu.SemaphoreType.DMA((units,)),
         ],
-        compiler_params=pltpu.CompilerParams(vmem_limit_bytes=14 * 2**20),
+        compiler_params=pltpu.CompilerParams(vmem_limit_bytes=18 * 2**20),
     )(own, other, pick, weight, *kept)
 
 

time: 203 us -> 202 us (level)
  no operation moved by 1% of the time
where the time goes in v3:
time: 202 us
  Pallas kernels  202 us (100%)
    pallas_call x1, Pallas kernels, exchange(): pl.pallas_call(functools.partial(exchange_kernel, early, late), in_specs=...  191 us
    pallas_call x1, Pallas kernels, finish(): pl.pallas_call(finish_kernel, in_specs=[vmem] * (4 + len(kept)), out_spec...  11 us

profile of v3, /device:TPU:0, one launch (start us, length us, event | category | flops | bytes accessed | tf_op | source)
XLA Modules:
  0.0 201.8 jit_solution(9867157172425728259)
XLA Ops:
  0.0 190.6 %shard_map.100 = (bf16[8,2,6,2,2,16,128]{6,5,4,3,2,1,0:T(8,128)(2,1)S(1)}, bf16[8,2,6,2,2,16,128]{6,5,4,3,2,1,0:T(8,128)(2,1)S(1)}, bf16[1024,256]{1,0:T(8,128)(...) custom-call(bf16[2,128,8192]{2,1,0:T(8,128)(2,1)} %bitcast.2, ...), custom_call_target="tpu_custom_call" | custom-call | flops 16000000000 | bytes 33554432 | tf_op jit(solution)/shard_map/pallas_call | solution.py:466
  190.6 11.0 %shard_map.101 = f32[8,32,2,2,64,128]{5,4,3,2,1,0:T(8,128)} custom-call(bf16[8,2,6,2,2,16,128]{6,5,4,3,2,1,0:T(8,128)(2,1)S(1)} %get-tuple-element.14.own, bf16[8,2,6,2,2,16,128]{6,5,4,3,2,1,0:T(8,128)(2,1)S(1)} %get-tuple-element.15.other, bf16[1024,256]{1,0:T(8,128)(2,1)S(1)} %get-tuple-element.16.pick, ...), custom_call_target="tpu_custom_call" | custom-call | tf_op jit(solution)/shard_map/pallas_call | solution.py:558

commit v4 on v3

--- a/solution.py
+++ b/solution.py
@@ -456,7 +456,7 @@
     high = matrix.astype(ml_dtypes.bfloat16)
     low = (matrix - high.astype(np.float64)).astype(ml_dtypes.bfloat16)
     early = [0, inside, units]
-    late = [0, inside * 2 // 5, inside * 4 // 5, inside, units - 2, units - 1, units]
+    late = [0, inside * 2 // 5, inside * 4 // 5, inside, units - 3, units - 1, units]
     count = max(len(early), len(late)) - 1
     shape = lambda count: (owners, chunks, count, halves, 2, BLOCK, depth)
     vmem = pl.BlockSpec(memory_space=pltpu.VMEM)

time: 202 us -> 202 us (level)
  no operation moved by 1% of the time
where the time goes in v4:
time: 202 us
  Pallas kernels  202 us (100%)
    pallas_call x1, Pallas kernels, exchange(): pl.pallas_call(functools.partial(exchange_kernel, early, late), in_specs=...  191 us
    pallas_call x1, Pallas kernels, finish(): pl.pallas_call(finish_kernel, in_specs=[vmem] * (4 + len(kept)), out_spec...  11 us

profile of v4, /device:TPU:0, one launch (start us, length us, event | category | flops | bytes accessed | tf_op | source)
XLA Modules:
  0.0 201.9 jit_solution(7733141794397305523)
XLA Ops:
  0.0 190.7 %shard_map.100 = (bf16[8,2,6,2,2,16,128]{6,5,4,3,2,1,0:T(8,128)(2,1)S(1)}, bf16[8,2,6,2,2,16,128]{6,5,4,3,2,1,0:T(8,128)(2,1)S(1)}, bf16[1024,256]{1,0:T(8,128)(...) custom-call(bf16[2,128,8192]{2,1,0:T(8,128)(2,1)} %bitcast.2, ...), custom_call_target="tpu_custom_call" | custom-call | flops 16000000000 | bytes 33554432 | tf_op jit(solution)/shard_map/pallas_call | solution.py:466
  190.7 11.0 %shard_map.101 = f32[8,32,2,2,64,128]{5,4,3,2,1,0:T(8,128)} custom-call(bf16[8,2,6,2,2,16,128]{6,5,4,3,2,1,0:T(8,128)(2,1)S(1)} %get-tuple-element.14.own, bf16[8,2,6,2,2,16,128]{6,5,4,3,2,1,0:T(8,128)(2,1)S(1)} %get-tuple-element.15.other, bf16[1024,256]{1,0:T(8,128)(2,1)S(1)} %get-tuple-element.16.pick, ...), custom_call_target="tpu_custom_call" | custom-call | tf_op jit(solution)/shard_map/pallas_call | solution.py:558
